TPU v7x, 32 devices: a whole 2x2x4 slice. The times are simulated.
32 devices in a mesh: feat: 8 (over z, y), dp: 4 (over x, core).
Axes of the slice: x: 2, y: 2, z: 4, core: 2. Of those that a mesh axis runs over, the one named last changes fastest.
Arguments:
- query_grads: bfloat16 [64, 131072], P(('dp', 'feat')), may hold values from -52 to 52
- build_grads: bfloat16 [512, 131072], P('dp', 'feat'), may hold values from -52 to 52
- scored_grads: bfloat16 [2048, 131072], P('dp', 'feat'), may hold values from -52 to 52
Outputs:
- scores: float32 [2048, 64], P(('dp', 'feat'))
All inputs are finite; a program needn't handle non-finite values.
Results may differ from a plain program's by a relative error of at most 0.0049.
Values may be sent and summed in bfloat16 or wider, within the bound.
A program may use at most 128 MiB of HBM per device.

v0:
```python
import functools

import jax
import jax.numpy as jnp
from jax import lax
from jax.experimental import pallas as pl
from jax.experimental.pallas import tpu as pltpu
from jax.sharding import PartitionSpec as P

BLOCK = 128
GROUP = 8


def contract_last(left, right):
    return lax.dot_general(
        left, right, (((1,), (1,)), ((), ())), preferred_element_type=jnp.float32
    )


def wide_dot(left, right, dims):
    return lax.dot_general(
        left,
        right,
        (dims, ((), ())),
        precision=lax.Precision.HIGHEST,
        preferred_element_type=jnp.float32,
    )


def invert_block(block):
    size = block.shape[0]
    lane = lax.broadcasted_iota(jnp.int32, (1, size), 1)
    row_id = lax.broadcasted_iota(jnp.int32, (size, 1), 0)

    def group(_, values):
        for k in range(GROUP):
            pivot = 1.0 / values[k : k + 1, k : k + 1]
            row = jnp.where(lane == k, pivot, values[k : k + 1, :] * pivot)
            column = jnp.where(row_id == k, -1.0, values[:, k : k + 1])
            base = jnp.where((lane == k) | (row_id == k), 0.0, values)
            values = base - column * row
        values = pltpu.roll(values, size - GROUP, 1)
        return jnp.concatenate([values[GROUP:], values[:GROUP]], axis=0)

    return lax.fori_loop(0, size // GROUP, group, block)


def solve_kernel(count, query_count, feature_count, tiles_ref, half_ref, scale_ref, work, cross, right):
    build_count = count * BLOCK
    place = {}
    for i in range(count):
        for j in range(i, count):
            place[i, j] = len(place)
    eye = lax.broadcasted_iota(jnp.int32, (BLOCK, BLOCK), 0) == lax.broadcasted_iota(
        jnp.int32, (BLOCK, BLOCK), 1
    )
    diagonal = jnp.zeros((BLOCK, BLOCK), jnp.float32)
    for i in range(count):
        diagonal = diagonal + jnp.where(eye, tiles_ref[place[i, i]], 0.0)
    total = jnp.sum(jnp.sum(diagonal, axis=1, keepdims=True), axis=0, keepdims=True)
    damping = 0.1 * total / (build_count * feature_count) + 1e-06
    shift = jnp.where(eye, build_count * damping, 0.0)
    for key, at in place.items():
        tile = tiles_ref[at]
        work[at] = tile + shift if key[0] == key[1] else tile
    width = right.shape[1] // BLOCK
    for i in range(count):
        for j in range(width):
            tile = tiles_ref[len(place) + i * width + j]
            cross[i * BLOCK : (i + 1) * BLOCK, j * BLOCK : (j + 1) * BLOCK] = tile
    right[...] = cross[...]

    def rows(i):
        return slice(i * BLOCK, (i + 1) * BLOCK)

    for k in range(count):
        inverse = invert_block(work[place[k, k]])
        solved_right = wide_dot(inverse, right[rows(k), :], ((1,), (0,)))
        scaled = {
            j: wide_dot(inverse, work[place[k, j]], ((1,), (0,))) for j in range(k + 1, count)
        }
        for i in range(k + 1, count):
            left = work[place[k, i]]
            for j in range(i, count):
                work[place[i, j]] -= wide_dot(left, scaled[j], ((0,), (0,)))
            right[rows(i), :] -= wide_dot(left, solved_right, ((0,), (0,)))
        for j in range(k + 1, count):
            work[place[k, j]] = scaled[j]
        right[rows(k), :] = solved_right
    for k in reversed(range(count - 1)):
        value = right[rows(k), :]
        for j in range(k + 1, count):
            value = value - wide_dot(work[place[k, j]], right[rows(j), :], ((1,), (0,)))
        right[rows(k), :] = value
    half = right[...].astype(jnp.bfloat16)
    half_ref[...] = half
    taken = jnp.sum(half.astype(jnp.float32) * cross[...], axis=0, keepdims=True)
    last = len(place) + count * width
    for j in range(width):
        lanes = slice(j * BLOCK, (j + 1) * BLOCK)
        kept = tiles_ref[last][j : j + 1, :] - taken[:, lanes]
        scale_ref[:, lanes] = 1.0 / jnp.sqrt(damping * kept)


def solve(tiles, build_count, query_count, feature_count):
    count = build_count // BLOCK
    wide = -(-query_count // BLOCK) * BLOCK
    pair_count = count * (count + 1) // 2
    vmem = pl.BlockSpec(memory_space=pltpu.VMEM)
    return pl.pallas_call(
        functools.partial(solve_kernel, count, query_count, feature_count),
        out_shape=(
            jax.ShapeDtypeStruct((build_count, wide), jnp.bfloat16),
            jax.ShapeDtypeStruct((1, wide), jnp.float32),
        ),
        in_specs=[vmem],
        out_specs=(vmem, vmem),
        scratch_shapes=[
            pltpu.VMEM((pair_count, BLOCK, BLOCK), jnp.float32),
            pltpu.VMEM((build_count, wide), jnp.float32),
            pltpu.VMEM((build_count, wide), jnp.float32),
        ],
        compiler_params=pltpu.CompilerParams(vmem_limit_bytes=48 * 1024 * 1024),
    )(tiles)


MESH = pl.DeviceIdType.MESH


def scatter_sum(values, axis, parts):
    split = values.reshape((parts, values.shape[0] // parts) + values.shape[1:])
    return jnp.sum(lax.all_to_all(split, axis, 0, 0), axis=0)


def exchange_kernel(
    feat_parts, dp_parts, query_ref, build_ref, query_out, build_out,
    local_sem, query_send, query_recv, build_send, build_recv,
):
    feat, dp = lax.axis_index("feat"), lax.axis_index("dp")
    parts = feat_parts * dp_parts
    me = dp * feat_parts + feat
    rows, span = build_ref.shape[0], build_out.shape[1]

    def peer(step):
        at = lax.rem(me + step, parts)
        return at, {"dp": at // feat_parts, "feat": lax.rem(at, feat_parts)}

    barrier = pltpu.get_barrier_semaphore()

    def greet(step, _):
        pl.semaphore_signal(barrier, inc=1, device_id=peer(step)[1], device_id_type=MESH)
        return 0

    lax.fori_loop(1, parts, greet, 0)
    pl.semaphore_wait(barrier, parts - 1)

    def query_copy(step):
        at, device = peer(step)
        return pltpu.make_async_remote_copy(
            src_ref=query_ref.at[at],
            dst_ref=query_out.at[me],
            send_sem=query_send.at[step],
            recv_sem=query_recv.at[step],
            device_id=device,
            device_id_type=MESH,
        )

    def columns(owner):
        return pl.ds(pl.multiple_of(owner * span, BLOCK), span)

    mine = pl.ds(pl.multiple_of(dp * rows, 16), rows)
    own = [
        pltpu.make_async_copy(build_ref.at[:, columns(dp)], build_out.at[mine], local_sem.at[0]),
        pltpu.make_async_copy(query_ref.at[me], query_out.at[me], local_sem.at[1]),
    ]
    sent = []
    for step in range(1, dp_parts):
        target = lax.rem(dp + step, dp_parts)
        sent.append(
            pltpu.make_async_remote_copy(
                src_ref=build_ref.at[:, columns(target)],
                dst_ref=build_out.at[mine],
                send_sem=build_send.at[step],
                recv_sem=build_recv.at[step],
                device_id={"dp": target, "feat": feat},
                device_id_type=MESH,
            )
        )

    def start_query(step, _):
        query_copy(step).start()
        return 0

    lax.fori_loop(1, parts, start_query, 0)
    for copy in sent + own:
        copy.start()

    def wait_query(step, _):
        query_copy(step).wait()
        return 0

    lax.fori_loop(1, parts, wait_query, 0)
    for copy in sent + own:
        copy.wait()


def exchange(query_grads, build_grads, feat_parts, dp_parts):
    parts = feat_parts * dp_parts
    rows, features = query_grads.shape
    span = features // parts
    arranged = query_grads.reshape(rows, feat_parts, dp_parts, span).transpose(2, 1, 0, 3)
    arranged = arranged.reshape(parts, rows * span // BLOCK, BLOCK)
    anywhere = pl.BlockSpec(memory_space=pl.ANY)
    query_out, build_out = pl.pallas_call(
        functools.partial(exchange_kernel, feat_parts, dp_parts),
        out_shape=(
            jax.ShapeDtypeStruct(arranged.shape, jnp.bfloat16),
            jax.ShapeDtypeStruct((build_grads.shape[0] * dp_parts, span), jnp.bfloat16),
        ),
        in_specs=[anywhere] * 2,
        out_specs=(anywhere, anywhere),
        scratch_shapes=[
            pltpu.SemaphoreType.DMA((2,)),
            pltpu.SemaphoreType.DMA((parts,)),
            pltpu.SemaphoreType.DMA((parts,)),
            pltpu.SemaphoreType.DMA((dp_parts,)),
            pltpu.SemaphoreType.DMA((dp_parts,)),
        ],
        compiler_params=pltpu.CompilerParams(collective_id=0, has_side_effects=True),
    )(arranged, build_grads)
    return query_out.reshape(rows * parts, span), build_out


def gram_kernel(query_ref, build_ref, out_ref, gram, cross, square):
    build_count, features = build_ref.shape
    query_count = query_ref.shape[0]
    count = build_count // BLOCK
    step = min(512, features)
    strip = 2 * BLOCK if count % 2 == 0 else BLOCK
    gram[...] = jnp.zeros_like(gram)
    cross[...] = jnp.zeros_like(cross)
    square[...] = jnp.zeros_like(square)

    @pl.loop(0, features // step)
    def _(at):
        here = pl.ds(pl.multiple_of(at * step, BLOCK), step)
        build = build_ref[:, here]
        query = query_ref[:, here]
        for low in range(0, build_count, strip):
            gram[low : low + strip, low:] += contract_last(build[low : low + strip], build[low:])
        cross[:, :query_count] += contract_last(build, query)
        wide = query.astype(jnp.float32)
        square[...] += jnp.sum(wide * wide, axis=1, keepdims=True)

    place = 0
    for i in range(count):
        for j in range(i, count):
            out_ref[pl.ds(place * BLOCK, BLOCK), :] = gram[
                i * BLOCK : (i + 1) * BLOCK, j * BLOCK : (j + 1) * BLOCK
            ]
            place += 1
    width = cross.shape[1] // BLOCK
    for i in range(count):
        for j in range(width):
            out_ref[pl.ds(place * BLOCK, BLOCK), :] = cross[
                i * BLOCK : (i + 1) * BLOCK, j * BLOCK : (j + 1) * BLOCK
            ]
            place += 1
    out_ref[pl.ds(place * BLOCK, out_ref.shape[0] - place * BLOCK), :] = jnp.zeros(
        (out_ref.shape[0] - place * BLOCK, BLOCK), jnp.float32
    )
    for j in range(-(-query_count // BLOCK)):
        size = min(BLOCK, query_count - j * BLOCK)
        eye = lax.broadcasted_iota(jnp.int32, (size, BLOCK), 0) == lax.broadcasted_iota(
            jnp.int32, (size, BLOCK), 1
        )
        column = square[j * BLOCK : j * BLOCK + size, :]
        row = jnp.sum(jnp.where(eye, column, 0.0), axis=0, keepdims=True)
        out_ref[pl.ds(place * BLOCK + j, 1), :] = row


def gram_tiles(query_local, build_local, tile_count):
    build_count, query_count = build_local.shape[0], query_local.shape[0]
    wide = -(-query_count // BLOCK) * BLOCK
    vmem = pl.BlockSpec(memory_space=pltpu.VMEM)
    return pl.pallas_call(
        gram_kernel,
        out_shape=jax.ShapeDtypeStruct((tile_count * BLOCK, BLOCK), jnp.float32),
        in_specs=[vmem] * 2,
        out_specs=vmem,
        scratch_shapes=[
            pltpu.VMEM((build_count, build_count), jnp.float32),
            pltpu.VMEM((build_count, wide), jnp.float32),
            pltpu.VMEM((query_count, 1), jnp.float32),
        ],
        compiler_params=pltpu.CompilerParams(vmem_limit_bytes=48 * 1024 * 1024),
    )(query_local, build_local)


def sum_kernel(
    feat_parts, dp_parts, values_ref, whole_ref,
    pair_in, pair_sum, chip_in, chip_sum, feat_in, send_sem, recv_sem,
):
    feat, dp = lax.axis_index("feat"), lax.axis_index("dp")
    chips = dp_parts // 2
    core, chip = lax.rem(dp, 2), dp // 2
    total = values_ref.shape[0]
    half, quarter, piece = total // 2, total // dp_parts, total // (dp_parts * feat_parts)

    def part(start, size):
        return pl.ds(pl.multiple_of(start, 8), size)

    other = {"dp": chip * 2 + 1 - core, "feat": feat}

    def along_chips(step):
        at = lax.rem(chip + step, chips)
        return at, {"dp": at * 2 + core, "feat": feat}

    def along_feat(step):
        at = lax.rem(feat + step, feat_parts)
        return at, {"dp": dp, "feat": at}

    barrier = pltpu.get_barrier_semaphore()
    peers = [other]
    peers += [along_chips(step)[1] for step in range(1, chips)]
    peers += [along_feat(step)[1] for step in range(1, feat_parts)]
    for device in peers:
        pl.semaphore_signal(barrier, inc=1, device_id=device, device_id_type=MESH)
    pl.semaphore_wait(barrier, len(peers))

    used = [0]

    def send(source, target, device):
        copy = pltpu.make_async_remote_copy(
            src_ref=source,
            dst_ref=target,
            send_sem=send_sem.at[used[0]],
            recv_sem=recv_sem.at[used[0]],
            device_id=device,
            device_id_type=MESH,
        )
        used[0] += 1
        copy.start()
        return copy

    send(values_ref.at[part((1 - core) * half, half)], pair_in, other).wait()
    pair_sum[...] = values_ref[part(core * half, half), :] + pair_in[...]

    copies = []
    for step in range(1, chips):
        at, device = along_chips(step)
        copies.append(send(pair_sum.at[part(at * quarter, quarter)], chip_in.at[step - 1], device))
    value = pair_sum[part(chip * quarter, quarter), :]
    for step, copy in enumerate(copies):
        copy.wait()
        value = value + chip_in[step]
    chip_sum[...] = value

    copies = []
    for step in range(1, feat_parts):
        at, device = along_feat(step)
        copies.append(send(chip_sum.at[part(at * piece, piece)], feat_in.at[step - 1], device))
    value = chip_sum[part(feat * piece, piece), :]
    for step, copy in enumerate(copies):
        copy.wait()
        value = value + feat_in[step]

    base = core * half + chip * quarter
    mine = whole_ref.at[part(base + feat * piece, piece)]
    mine[...] = value
    copies = [send(mine, mine, along_feat(step)[1]) for step in range(1, feat_parts)]
    for copy in copies:
        copy.wait()
    mine = whole_ref.at[part(base, quarter)]
    copies = [send(mine, mine, along_chips(step)[1]) for step in range(1, chips)]
    for copy in copies:
        copy.wait()
    mine = whole_ref.at[part(core * half, half)]
    send(mine, mine, other).wait()


def sum_everywhere(values, feat_parts, dp_parts):
    total = values.shape[0]
    chips = dp_parts // 2
    quarter, piece = total // dp_parts, total // (dp_parts * feat_parts)
    copies = 2 * (1 + (chips - 1) + (feat_parts - 1))
    vmem = pl.BlockSpec(memory_space=pltpu.VMEM)
    return pl.pallas_call(
        functools.partial(sum_kernel, feat_parts, dp_parts),
        out_shape=jax.ShapeDtypeStruct(values.shape, jnp.float32),
        in_specs=[vmem],
        out_specs=vmem,
        scratch_shapes=[
            pltpu.VMEM((total // 2, BLOCK), jnp.float32),
            pltpu.VMEM((total // 2, BLOCK), jnp.float32),
            pltpu.VMEM((max(1, chips - 1), quarter, BLOCK), jnp.float32),
            pltpu.VMEM((quarter, BLOCK), jnp.float32),
            pltpu.VMEM((max(1, feat_parts - 1), piece, BLOCK), jnp.float32),
            pltpu.SemaphoreType.DMA((copies,)),
            pltpu.SemaphoreType.DMA((copies,)),
        ],
        compiler_params=pltpu.CompilerParams(
            collective_id=1, has_side_effects=True, vmem_limit_bytes=48 * 1024 * 1024
        ),
    )(values)


def on_device(feat_parts, dp_parts, query_grads, build_grads, scored_grads):
    feature_count = query_grads.shape[1]
    q_local, b_local = exchange(query_grads, build_grads, feat_parts, dp_parts)
    build_count, query_count = b_local.shape[0], q_local.shape[0]
    count, width = build_count // BLOCK, -(-query_count // BLOCK)
    used = count * (count + 1) // 2 + count * width + 1
    unit = max(1, feat_parts * dp_parts // 16)
    tile_count = -(-used // unit) * unit
    tiles = gram_tiles(q_local, b_local, tile_count)
    whole = sum_everywhere(tiles, feat_parts, dp_parts).reshape(tile_count, BLOCK, BLOCK)
    solved_half, scale = solve(whole, build_count, query_count, feature_count)
    query_wide = q_local.astype(jnp.float32)
    removed = lax.dot_general(
        solved_half[:, :query_count], b_local, (((0,), (0,)), ((), ())),
        preferred_element_type=jnp.float32,
    )
    normed = ((query_wide - removed) * scale[:, :query_count].reshape(-1, 1)).astype(jnp.bfloat16)
    normed = lax.all_gather(normed, "dp", axis=1, tiled=True)
    partial_value = contract_last(scored_grads, normed)
    return scatter_sum(partial_value, "feat", feat_parts)


def solution(mesh):
    placed = (P(("dp", "feat"), None), P("dp", "feat"), P("dp", "feat"))
    return jax.shard_map(
        functools.partial(on_device, mesh.shape["feat"], mesh.shape["dp"]),
        mesh=mesh,
        in_specs=placed,
        out_specs=P(("dp", "feat"), None),
        check_vma=False,
    )
```

profile of v0, /device:TPU:0, one launch (start us, length us, event | category | flops | bytes accessed | tf_op | source)
XLA Modules:
  0.0 217.3 jit_solution(5936547273898840108)
XLA Ops:
  6.5 0.0 all-gather.2.cloned.1.call-start
  6.5 1.4 reshape.17
  7.9 0.5 copy.12
  8.5 1.2 reshape.18.query_ref
  9.7 59.0 %shard_map.37 = (bf16[32,64,128]{2,1,0:T(8,128)(2,1)}, bf16[512,4096]{1,0:T(8,128)(2,1)}) custom-call(bf16[32,64,128]{2,1,0:T(8,128)(2,1)} %reshape.18.query_ref, bf16[128,16384]{1,0:T(8,128)(2,1)} %build_ref.1), custom_call_target="tpu_custom_call" | custom-call | tf_op jit(solution)/shard_map/pallas_call | solution.py:214
  68.7 1.3 reshape.19.query_ref
  70.0 0.0 copy-start
  70.0 2.2 %copy-done = bf16[512,4096]{1,0:T(8,128)(2,1)S(1)} copy-done((bf16[512,4096]{1,0:T(8,128)(2,1)S(1)}, bf16[512,4096]{1,0:T(8,128)(2,1)}, u32[]{:S(2)}) %copy-start) | copy-done | bytes 4194328
  72.2 0.0 copy-start.1
  72.2 4.5 %shard_map.38.values_ref = f32[2048,128]{1,0:T(8,128)S(1)} custom-call(bf16[64,4096]{1,0:T(8,128)(2,1)S(1)} %reshape.19.query_ref, bf16[512,4096]{1,0:T(8,128)(2,1)S(1)} %copy-done), custom_call_target="tpu_custom_call" | custom-call | tf_op jit(solution)/shard_map/pallas_call | solution.py:286
  76.7 30.8 %shard_map.39 = f32[2048,128]{1,0:T(8,128)S(1)} custom-call(f32[2048,128]{1,0:T(8,128)S(1)} %shard_map.38.values_ref), custom_call_target="tpu_custom_call" | custom-call | tf_op jit(solution)/shard_map/pallas_call | solution.py:388
  107.4 51.0 %shard_map.40 = (bf16[512,128]{1,0:T(8,128)(2,1)S(1)}, f32[1,128]{1,0:T(1,128)S(1)}) custom-call(f32[16,128,128]{2,1,0:T(8,128)S(1)} %bitcast.18), custom_call_target="tpu_custom_call" | custom-call | tf_op jit(solution)/shard_map/pallas_call | solution.py:110
  158.5 0.0 copy-done.1
  158.5 1.7 fusion.1
  160.2 0.0 all-gather.2.cloned.1.call-update
  160.2 23.3 %all-gather.2.cloned.1.call-done = bf16[64,16384]{1,0:T(8,128)(2,1)} async-done(((bf16[64,4096]{1,0:T(8,128)(2,1)}), bf16[64,16384]{1,0:T(8,128)(2,1)}) %all-gather.2.cloned.1.call-update) | async-done | bytes 2097168 | tf_op jit(solution)/shard_map/all_gather | solution.py:425
  183.5 11.6 %convolution_bitcast_fusion = f32[512,64]{0,1:T(8,128)S(1)} fusion(bf16[64,16384]{1,0:T(8,128)(2,1)} %all-gather.2.cloned.1.call-done, bf16[512,16384]{1,0:T(8,128)(2,1)} %param.5), kind=kOutput, calls=%fused_computation.3 | convolution fusion | flops 1073741824 | bytes 19005440 | tf_op jit(solution)/shard_map/dot_general | solution.py:15
  195.1 0.1 reshape.21
  195.2 0.1 copy.13
  195.3 0.2 reshape.22
  195.5 12.7 %all_to_all.5 = f32[8,1,4096]{2,1,0:T(1,128)S(1)} all-to-all(f32[8,1,4096]{2,1,0:T(1,128)S(1)} %reshape.22), channel_id=1, replica_groups=mesh['feat'=8,'dp'=4] {'feat'}, dimensions={0} | all-to-all | bytes 262144 | tf_op jit(solution)/shard_map/all_to_all | solution.py:132
  208.2 0.5 broadcast
  208.7 1.0 reduce
  209.6 0.1 reshape.23
  209.8 0.7 copy.8
  (2 shorter events, 0.0 us)
Async XLA Ops:
  6.5 177.0 %all-gather.2.cloned.1.call-start = ((), (), s32[]{:S(2)}) async-start(), calls=%async_computation.1 | async-start | bytes 2621440 | tf_op jit(solution)/shard_map/all_gather | solution.py:425
  70.0 2.2 %copy-start = (bf16[512,4096]{1,0:T(8,128)(2,1)S(1)}, bf16[512,4096]{1,0:T(8,128)(2,1)}, u32[]{:S(2)}) copy-start(bf16[512,4096]{1,0:T(8,128)(2,1)} %get-tuple-element.10.build_ref) | copy-start | bytes 12582916
  72.2 86.3 %copy-start.1 = (bf16[512,4096]{1,0:T(8,128)(2,1)S(1)}, bf16[512,4096]{1,0:T(8,128)(2,1)}, u32[]{:S(2)}) copy-start(bf16[512,4096]{1,0:T(8,128)(2,1)} %get-tuple-element.10.build_ref) | copy-start | bytes 12582916
Sparse Core Ops, SparseCore 0:
  160.3 23.1 all-gather.1
where the time goes:
time: 218 us; the launch traced here: 217 us
  Pallas kernels  145 us (67%)
  waiting for transfers between devices  23.4 us (11%)
  between operations  13.5 us (6%)
  matrix products  13.3 us (6%)
  blocking collectives  12.7 us (6%)
  local copies, waits for them, and re-layouts  8.21 us (4%)
    pallas_call x1, Pallas kernels, exchange(): pl.pallas_call(functools.partial(exchange_kernel, feat_parts, dp_parts),...  59 us
    pallas_call x1, Pallas kernels, solve(): pl.pallas_call(functools.partial(solve_kernel, count, query_count, featur...  51 us
    pallas_call x1, Pallas kernels, sum_everywhere(): pl.pallas_call(functools.partial(sum_kernel, feat_parts, dp_parts), out_s...  30.8 us
    all_gather x1, waiting for transfers between devices, on_device(): normed = lax.all_gather(normed, 'dp', axis=1, tiled=True)  23.3 us
    all_to_all x1, blocking collectives, scatter_sum(): return jnp.sum(lax.all_to_all(split, axis, 0, 0), axis=0)  12.7 us
    dot_general x1, matrix products, contract_last(): lax.dot_general(left, right, (((1,), (1,)), ((), ())), preferred_element_...  11.6 us
    pallas_call x1, Pallas kernels, gram_tiles(): pl.pallas_call(gram_kernel, out_shape=jax.ShapeDtypeStruct((tile_count *...  4.5 us
  transfers between devices with their start and end apart: 1, of which 1 were waited for; matrix products, arithmetic and copies ran while one was open for 0% of the time, Pallas kernels for 0%

commit v1 on v0

--- a/solution.py
+++ b/solution.py
@@ -30,23 +30,35 @@
 def invert_block(block):
     size = block.shape[0]
     lane = lax.broadcasted_iota(jnp.int32, (1, size), 1)
-    row_id = lax.broadcasted_iota(jnp.int32, (size, 1), 0)
+    row_id = lax.broadcasted_iota(jnp.int32, (GROUP, 1), 0)
 
     def group(_, values):
-        for k in range(GROUP):
-            pivot = 1.0 / values[k : k + 1, k : k + 1]
-            row = jnp.where(lane == k, pivot, values[k : k + 1, :] * pivot)
-            column = jnp.where(row_id == k, -1.0, values[:, k : k + 1])
-            base = jnp.where((lane == k) | (row_id == k), 0.0, values)
-            values = base - column * row
-        values = pltpu.roll(values, size - GROUP, 1)
-        return jnp.concatenate([values[GROUP:], values[:GROUP]], axis=0)
+        top, rest = values[:GROUP], values[GROUP:]
+        for k in range(0, GROUP, 2):
+            first, second = lane == k, lane == k + 1
+            top_0, top_1 = top[:, k : k + 1], top[:, k + 1 : k + 2]
+            rest_0, rest_1 = rest[:, k : k + 1], rest[:, k + 1 : k + 2]
+            corner, upper = top_0[k : k + 1], top_1[k : k + 1]
+            lower, other = top_0[k + 1 : k + 2], top_1[k + 1 : k + 2]
+            inverse = 1.0 / (corner * other - upper * lower)
+            row_0 = jnp.where(first, 1.0, jnp.where(second, 0.0, top[k : k + 1]))
+            row_1 = jnp.where(first, 0.0, jnp.where(second, 1.0, top[k + 1 : k + 2]))
+            new_0 = (other * row_0 - upper * row_1) * inverse
+            new_1 = (corner * row_1 - lower * row_0) * inverse
+            both = first | second
+            at_0, at_1 = row_id == k, row_id == k + 1
+            top_0 = jnp.where(at_0, -1.0, jnp.where(at_1, 0.0, top_0))
+            top_1 = jnp.where(at_1, -1.0, jnp.where(at_0, 0.0, top_1))
+            top = jnp.where(both | at_0 | at_1, 0.0, top) - top_0 * new_0 - top_1 * new_1
+            rest = jnp.where(both, 0.0, rest) - rest_0 * new_0 - rest_1 * new_1
+        return pltpu.roll(jnp.concatenate([rest, top], axis=0), size - GROUP, 1)
 
     return lax.fori_loop(0, size // GROUP, group, block)
 
 
-def solve_kernel(count, query_count, feature_count, tiles_ref, half_ref, scale_ref, work, cross, right):
+def solve_kernel(count, feature_count, tiles_ref, half_ref, scale_ref, right, *strips):
     build_count = count * BLOCK
+    width = right.shape[1] // BLOCK
     place = {}
     for i in range(count):
         for j in range(i, count):
@@ -60,76 +72,65 @@
     total = jnp.sum(jnp.sum(diagonal, axis=1, keepdims=True), axis=0, keepdims=True)
     damping = 0.1 * total / (build_count * feature_count) + 1e-06
     shift = jnp.where(eye, build_count * damping, 0.0)
-    for key, at in place.items():
-        tile = tiles_ref[at]
-        work[at] = tile + shift if key[0] == key[1] else tile
-    width = right.shape[1] // BLOCK
+
+    def lanes(i):
+        return slice(i * BLOCK, (i + 1) * BLOCK)
+
     for i in range(count):
+        for j in range(i, count):
+            tile = tiles_ref[place[i, j]]
+            strips[i][:, lanes(j - i)] = tile + shift if i == j else tile
         for j in range(width):
-            tile = tiles_ref[len(place) + i * width + j]
-            cross[i * BLOCK : (i + 1) * BLOCK, j * BLOCK : (j + 1) * BLOCK] = tile
-    right[...] = cross[...]
-
-    def rows(i):
-        return slice(i * BLOCK, (i + 1) * BLOCK)
+            strips[i][:, lanes(count - i + j)] = tiles_ref[len(place) + i * width + j]
 
     for k in range(count):
-        inverse = invert_block(work[place[k, k]])
-        solved_right = wide_dot(inverse, right[rows(k), :], ((1,), (0,)))
-        scaled = {
-            j: wide_dot(inverse, work[place[k, j]], ((1,), (0,))) for j in range(k + 1, count)
-        }
+        inverse = invert_block(strips[k][:, :BLOCK])
+        scaled = wide_dot(inverse, strips[k][:, BLOCK:], ((1,), (0,)))
         for i in range(k + 1, count):
-            left = work[place[k, i]]
-            for j in range(i, count):
-                work[place[i, j]] -= wide_dot(left, scaled[j], ((0,), (0,)))
-            right[rows(i), :] -= wide_dot(left, solved_right, ((0,), (0,)))
-        for j in range(k + 1, count):
-            work[place[k, j]] = scaled[j]
-        right[rows(k), :] = solved_right
-    for k in reversed(range(count - 1)):
-        value = right[rows(k), :]
-        for j in range(k + 1, count):
-            value = value - wide_dot(work[place[k, j]], right[rows(j), :], ((1,), (0,)))
-        right[rows(k), :] = value
+            left = strips[k][:, lanes(i - k)]
+            strips[i][...] -= wide_dot(left, scaled[:, (i - k - 1) * BLOCK :], ((0,), (0,)))
+        strips[k][:, BLOCK:] = scaled
+    for k in reversed(range(count)):
+        end = (count - k) * BLOCK
+        value = strips[k][:, end:]
+        if k + 1 < count:
+            value = value - wide_dot(
+                strips[k][:, BLOCK:end], right[(k + 1) * BLOCK :, :], ((1,), (0,))
+            )
+        right[k * BLOCK : (k + 1) * BLOCK, :] = value
     half = right[...].astype(jnp.bfloat16)
     half_ref[...] = half
-    taken = jnp.sum(half.astype(jnp.float32) * cross[...], axis=0, keepdims=True)
     last = len(place) + count * width
     for j in range(width):
-        lanes = slice(j * BLOCK, (j + 1) * BLOCK)
-        kept = tiles_ref[last][j : j + 1, :] - taken[:, lanes]
-        scale_ref[:, lanes] = 1.0 / jnp.sqrt(damping * kept)
+        taken = jnp.zeros((1, BLOCK), jnp.float32)
+        for i in range(count):
+            block = half[lanes(i), lanes(j)].astype(jnp.float32)
+            taken = taken + jnp.sum(
+                block * tiles_ref[len(place) + i * width + j], axis=0, keepdims=True
+            )
+        kept = tiles_ref[last][j : j + 1, :] - taken
+        scale_ref[:, lanes(j)] = 1.0 / jnp.sqrt(damping * kept)
 
 
 def solve(tiles, build_count, query_count, feature_count):
     count = build_count // BLOCK
     wide = -(-query_count // BLOCK) * BLOCK
-    pair_count = count * (count + 1) // 2
     vmem = pl.BlockSpec(memory_space=pltpu.VMEM)
     return pl.pallas_call(
-        functools.partial(solve_kernel, count, query_count, feature_count),
+        functools.partial(solve_kernel, count, feature_count),
         out_shape=(
             jax.ShapeDtypeStruct((build_count, wide), jnp.bfloat16),
             jax.ShapeDtypeStruct((1, wide), jnp.float32),
         ),
         in_specs=[vmem],
         out_specs=(vmem, vmem),
-        scratch_shapes=[
-            pltpu.VMEM((pair_count, BLOCK, BLOCK), jnp.float32),
-            pltpu.VMEM((build_count, wide), jnp.float32),
-            pltpu.VMEM((build_count, wide), jnp.float32),
-        ],
+        scratch_shapes=[pltpu.VMEM((build_count, wide), jnp.float32)]
+        + [pltpu.VMEM((BLOCK, (count - k) * BLOCK + wide), jnp.float32) for k in range(count)],
         compiler_params=pltpu.CompilerParams(vmem_limit_bytes=48 * 1024 * 1024),
     )(tiles)
 
 
 MESH = pl.DeviceIdType.MESH
-
-
-def scatter_sum(values, axis, parts):
-    split = values.reshape((parts, values.shape[0] // parts) + values.shape[1:])
-    return jnp.sum(lax.all_to_all(split, axis, 0, 0), axis=0)
 
 
 def exchange_kernel(
@@ -405,6 +406,188 @@
     )(values)
 
 
+def score_kernel(
+    feat_parts, dp_parts, half_ref, scale_ref, query_ref, build_ref, scored_ref, out_ref,
+    normed, scored, total, packed, arrived,
+    load_sem, pair_send, pair_recv, chip_send, chip_recv, pass_send, pass_recv, feat_send, feat_recv,
+):
+    feat, dp = lax.axis_index("feat"), lax.axis_index("dp")
+    chips = dp_parts // 2
+    core, chip = lax.rem(dp, 2), dp // 2
+    query_count, span = query_ref.shape
+    rows = scored_ref.shape[0]
+    pieces = normed.shape[0] // dp_parts
+    size = span // pieces
+    other = {"dp": chip * 2 + 1 - core, "feat": feat}
+
+    def along_chips(step):
+        return {"dp": lax.rem(chip + step, chips) * 2 + core, "feat": feat}
+
+    def from_chip(step):
+        return lax.rem(chip + chips - step, chips) * 2
+
+    def along_feat(step):
+        at = lax.rem(feat + step, feat_parts)
+        return at, {"dp": dp, "feat": at}
+
+    loads = []
+    owners = [dp, chip * 2 + 1 - core]
+    for step in range(1, chips):
+        owners += [from_chip(step) + core, from_chip(step) + 1 - core]
+    for at, owner in enumerate(owners):
+        columns = pl.ds(pl.multiple_of(owner * span, BLOCK), span)
+        load = pltpu.make_async_copy(scored_ref.at[:, columns], scored.at[at], load_sem.at[at])
+        load.start()
+        loads.append(load)
+
+    peers = [other] + [along_chips(step) for step in range(1, chips)]
+    peers += [along_feat(step)[1] for step in range(1, feat_parts)]
+    barrier = pltpu.get_barrier_semaphore()
+    for device in peers:
+        pl.semaphore_signal(barrier, inc=1, device_id=device, device_id_type=MESH)
+    pl.semaphore_wait(barrier, len(peers))
+
+    def send(slot, device, send_sem, recv_sem):
+        return pltpu.make_async_remote_copy(
+            src_ref=normed.at[slot],
+            dst_ref=normed.at[slot],
+            send_sem=send_sem,
+            recv_sem=recv_sem,
+            device_id=device,
+            device_id_type=MESH,
+        )
+
+    half = half_ref[:, :query_count]
+    scale_row = scale_ref[:, :query_count]
+    eye = lax.broadcasted_iota(jnp.int32, (query_count, query_count), 0) == lax.broadcasted_iota(
+        jnp.int32, (query_count, query_count), 1
+    )
+    scale = jnp.sum(jnp.where(eye, scale_row, 0.0), axis=1, keepdims=True)
+    sent, pairs, chip_copies = [], [], {}
+    for piece in range(pieces):
+        here = slice(piece * size, (piece + 1) * size)
+        removed = lax.dot_general(
+            half, build_ref[:, here], (((0,), (0,)), ((), ())), preferred_element_type=jnp.float32
+        )
+        value = (query_ref[:, here].astype(jnp.float32) - removed) * scale
+        normed[dp * pieces + piece] = value.astype(jnp.bfloat16)
+        for step in range(1, chips):
+            at = (step - 1) * pieces + piece
+            copy = send(dp * pieces + piece, along_chips(step), chip_send.at[at], chip_recv.at[at])
+            copy.start()
+            chip_copies[step, piece] = copy
+        copy = send(dp * pieces + piece, other, pair_send.at[piece], pair_recv.at[piece])
+        copy.start()
+        pairs.append(copy)
+
+    total[...] = jnp.zeros_like(total)
+
+    def multiply(at, piece):
+        left = scored.at[at]
+        right = normed.at[owners[at] * pieces + piece]
+
+        @pl.loop(0, rows // BLOCK)
+        def _(row):
+            here = pl.ds(pl.multiple_of(row * BLOCK, BLOCK), BLOCK)
+            total[here, :] += contract_last(
+                left[here, piece * size : (piece + 1) * size], right[...]
+            )
+
+    loads[0].wait()
+    for piece in range(pieces):
+        multiply(0, piece)
+    loads[1].wait()
+    for piece in range(pieces):
+        pairs[piece].wait_recv()
+        multiply(1, piece)
+    passed = []
+    for step in range(1, chips):
+        loads[2 * step].wait()
+        loads[2 * step + 1].wait()
+    for piece in range(pieces):
+        for step in range(1, chips):
+            at = (step - 1) * pieces + piece
+            chip_copies[step, piece].wait_recv()
+            copy = send(
+                (from_chip(step) + core) * pieces + piece, other, pass_send.at[at], pass_recv.at[at]
+            )
+            copy.start()
+            multiply(2 * step, piece)
+            copy.wait_recv()
+            multiply(2 * step + 1, piece)
+            passed.append(copy)
+    for copy in pairs + list(chip_copies.values()) + passed:
+        copy.wait_send()
+
+    share = rows // feat_parts
+    fold = packed.shape[2] // query_count
+    part = share // fold
+    for owner in range(feat_parts):
+        blocks = [
+            total[owner * share + at * part : owner * share + (at + 1) * part, :]
+            for at in range(fold)
+        ]
+        packed[owner] = blocks[0] if fold == 1 else jnp.concatenate(blocks, axis=1)
+    copies = []
+    for step in range(1, feat_parts):
+        at, device = along_feat(step)
+        copy = pltpu.make_async_remote_copy(
+            src_ref=packed.at[at],
+            dst_ref=arrived.at[step - 1],
+            send_sem=feat_send.at[step],
+            recv_sem=feat_recv.at[step],
+            device_id=device,
+            device_id_type=MESH,
+        )
+        copy.start()
+        copies.append(copy)
+    value = packed[feat]
+    for step, copy in enumerate(copies):
+        copy.wait()
+        value = value + arrived[step]
+    for at in range(fold):
+        out_ref[at * part : (at + 1) * part, :] = value[
+            :, at * query_count : (at + 1) * query_count
+        ]
+
+
+def score(solved_half, scale, query_local, build_local, scored_grads, feat_parts, dp_parts):
+    query_count, span = query_local.shape
+    rows = scored_grads.shape[0]
+    pieces = 2 if span % (2 * BLOCK) == 0 else 1
+    chips = dp_parts // 2
+    share = rows // feat_parts
+    fold = BLOCK // query_count if query_count < BLOCK and share % (8 * BLOCK // query_count) == 0 else 1
+    vmem = pl.BlockSpec(memory_space=pltpu.VMEM)
+    remote = max(1, (chips - 1) * pieces)
+    dma = pltpu.SemaphoreType.DMA
+    return pl.pallas_call(
+        functools.partial(score_kernel, feat_parts, dp_parts),
+        out_shape=jax.ShapeDtypeStruct((share, query_count), jnp.float32),
+        in_specs=[vmem] * 4 + [pl.BlockSpec(memory_space=pl.ANY)],
+        out_specs=vmem,
+        scratch_shapes=[
+            pltpu.VMEM((dp_parts * pieces, query_count, span // pieces), jnp.bfloat16),
+            pltpu.VMEM((dp_parts, rows, span), jnp.bfloat16),
+            pltpu.VMEM((rows, query_count), jnp.float32),
+            pltpu.VMEM((feat_parts, share // fold, query_count * fold), jnp.float32),
+            pltpu.VMEM((max(1, feat_parts - 1), share // fold, query_count * fold), jnp.float32),
+            dma((dp_parts,)),
+            dma((pieces,)),
+            dma((pieces,)),
+            dma((remote,)),
+            dma((remote,)),
+            dma((remote,)),
+            dma((remote,)),
+            dma((feat_parts,)),
+            dma((feat_parts,)),
+        ],
+        compiler_params=pltpu.CompilerParams(
+            collective_id=2, has_side_effects=True, vmem_limit_bytes=48 * 1024 * 1024
+        ),
+    )(solved_half, scale, query_local, build_local, scored_grads)
+
+
 def on_device(feat_parts, dp_parts, query_grads, build_grads, scored_grads):
     feature_count = query_grads.shape[1]
     q_local, b_local = exchange(query_grads, build_grads, feat_parts, dp_parts)
@@ -416,15 +599,7 @@
     tiles = gram_tiles(q_local, b_local, tile_count)
     whole = sum_everywhere(tiles, feat_parts, dp_parts).reshape(tile_count, BLOCK, BLOCK)
     solved_half, scale = solve(whole, build_count, query_count, feature_count)
-    query_wide = q_local.astype(jnp.float32)
-    removed = lax.dot_general(
-        solved_half[:, :query_count], b_local, (((0,), (0,)), ((), ())),
-        preferred_element_type=jnp.float32,
-    )
-    normed = ((query_wide - removed) * scale[:, :query_count].reshape(-1, 1)).astype(jnp.bfloat16)
-    normed = lax.all_gather(normed, "dp", axis=1, tiled=True)
-    partial_value = contract_last(scored_grads, normed)
-    return scatter_sum(partial_value, "feat", feat_parts)
+    return score(solved_half, scale, q_local, b_local, scored_grads, feat_parts, dp_parts)
 
 
 def solution(mesh):

time: 218 us -> 192 us (0.88)
  Pallas kernels: 145 us -> 184 us
  waiting for transfers between devices: 23.4 us -> 0 us
  between operations: 13.5 us -> 0.06 us
  matrix products: 13.3 us -> 0 us
  blocking collectives: 12.7 us -> 0 us
    pallas_call x1 -> x2, Pallas kernels: 51 us -> 89.8 us  [the longest x1 65.1 us: solve(): pl.pallas_call(functools.partial(solve_kernel, count, feature_count), out...]
    all_gather x1 -> x0, waiting for transfers between devices: 23.3 us -> none  [on_device(): normed = lax.all_gather(normed, 'dp', axis=1, tiled=True)]
    dot_general x2 -> x0, matrix products: 13.3 us -> none  [the longest x1 11.6 us: contract_last(): lax.dot_general(left, right, (((1,), (1,)), ((), ())), preferred_element_...]
    all_to_all x1 -> x0, blocking collectives: 12.7 us -> none  [scatter_sum(): return jnp.sum(lax.all_to_all(split, axis, 0, 0), axis=0)]
  transfers between devices with their start and end apart: 1 -> 0, of which waited for: 1 -> 0; matrix products, arithmetic and copies ran while one was open for 0% -> 0% of each run, Pallas kernels for 0% -> 0%
where the time goes in v1:
time: 192 us; the launch traced here: 191 us
  Pallas kernels  184 us (96%)
  local copies, waits for them, and re-layouts  7.18 us (4%)
    pallas_call x1, Pallas kernels, solve(): pl.pallas_call(functools.partial(solve_kernel, count, feature_count), out...  65.1 us
    pallas_call x1, Pallas kernels, exchange(): pl.pallas_call(functools.partial(exchange_kernel, feat_parts, dp_parts),...  59 us
    pallas_call x1, Pallas kernels, sum_everywhere(): pl.pallas_call(functools.partial(sum_kernel, feat_parts, dp_parts), out_s...  30.8 us
    pallas_call x1, Pallas kernels, score(): pl.pallas_call(functools.partial(score_kernel, feat_parts, dp_parts), out...  24.7 us
    pallas_call x1, Pallas kernels, gram_tiles(): pl.pallas_call(gram_kernel, out_shape=jax.ShapeDtypeStruct((tile_count *...  4.51 us

profile of v1, /device:TPU:0, one launch (start us, length us, event | category | flops | bytes accessed | tf_op | source)
XLA Modules:
  0.0 191.3 jit_solution(7461935480147234642)
XLA Ops:
  0.0 1.4 reshape.12
  1.4 0.5 copy.6
  1.9 1.2 reshape.13.query_ref
  3.1 59.0 %shard_map.37 = (bf16[32,64,128]{2,1,0:T(8,128)(2,1)}, bf16[512,4096]{1,0:T(8,128)(2,1)}) custom-call(bf16[32,64,128]{2,1,0:T(8,128)(2,1)} %reshape.13.query_ref, bf16[128,16384]{1,0:T(8,128)(2,1)} %build_ref.1), custom_call_target="tpu_custom_call" | custom-call | tf_op jit(solution)/shard_map/pallas_call | solution.py:215
  62.2 1.3 reshape.14.query_ref
  63.4 0.0 copy-start
  63.4 2.2 %copy-done = bf16[512,4096]{1,0:T(8,128)(2,1)S(1)} copy-done((bf16[512,4096]{1,0:T(8,128)(2,1)S(1)}, bf16[512,4096]{1,0:T(8,128)(2,1)}, u32[]{:S(2)}) %copy-start) | copy-done | bytes 4194328
  65.6 0.0 copy-start.1
  65.6 4.5 %shard_map.38.values_ref = f32[2048,128]{1,0:T(8,128)S(1)} custom-call(bf16[64,4096]{1,0:T(8,128)(2,1)S(1)} %reshape.14.query_ref, bf16[512,4096]{1,0:T(8,128)(2,1)S(1)} %copy-done), custom_call_target="tpu_custom_call" | custom-call | tf_op jit(solution)/shard_map/pallas_call | solution.py:287
  70.1 30.8 %shard_map.39 = f32[2048,128]{1,0:T(8,128)S(1)} custom-call(f32[2048,128]{1,0:T(8,128)S(1)} %shard_map.38.values_ref), custom_call_target="tpu_custom_call" | custom-call | tf_op jit(solution)/shard_map/pallas_call | solution.py:389
  100.9 65.1 %shard_map.40 = (bf16[512,128]{1,0:T(8,128)(2,1)S(1)}, f32[1,128]{1,0:T(1,128)S(1)}) custom-call(f32[16,128,128]{2,1,0:T(8,128)S(1)} %bitcast.4), custom_call_target="tpu_custom_call" | custom-call | tf_op jit(solution)/shard_map/pallas_call | solution.py:119
  166.0 0.0 copy-done.1
  166.0 24.7 %shard_map.41 = f32[64,64]{1,0:T(8,128)S(1)} custom-call(bf16[512,128]{1,0:T(8,128)(2,1)S(1)} %get-tuple-element.11.half_ref, f32[1,128]{1,0:T(1,128)S(1)} %get-tuple-element.12.scale_ref, bf16[64,4096]{1,0:T(8,128)(2,1)S(1)} %reshape.14.query_ref, bf16[512,4096]{1,0:T(8,128)(2,1)S(1)} %copy-done.1, bf16[512,16384]{1,0:T(8,128)(2,1)} %scored_ref.1), custom_call_target="tpu_custom_call" | custom-call | tf_op jit(solution)/shard_map/pallas_call | solution.py:564
  190.7 0.6 copy.8
Async XLA Ops:
  63.4 2.2 %copy-start = (bf16[512,4096]{1,0:T(8,128)(2,1)S(1)}, bf16[512,4096]{1,0:T(8,128)(2,1)}, u32[]{:S(2)}) copy-start(bf16[512,4096]{1,0:T(8,128)(2,1)} %get-tuple-element.10.build_ref) | copy-start | bytes 12582916
  65.6 100.4 %copy-start.1 = (bf16[512,4096]{1,0:T(8,128)(2,1)S(1)}, bf16[512,4096]{1,0:T(8,128)(2,1)}, u32[]{:S(2)}) copy-start(bf16[512,4096]{1,0:T(8,128)(2,1)} %get-tuple-element.10.build_ref) | copy-start | bytes 12582916

commit v2 on v1

--- a/solution.py
+++ b/solution.py
@@ -9,6 +9,7 @@
 
 BLOCK = 128
 GROUP = 8
+CHUNKS = 2
 
 
 def contract_last(left, right):
@@ -30,30 +31,32 @@
 def invert_block(block):
     size = block.shape[0]
     lane = lax.broadcasted_iota(jnp.int32, (1, size), 1)
-    row_id = lax.broadcasted_iota(jnp.int32, (GROUP, 1), 0)
+    row_id = lax.broadcasted_iota(jnp.int32, (GROUP, size), 0)
+    inside = lane < GROUP
 
     def group(_, values):
         top, rest = values[:GROUP], values[GROUP:]
-        for k in range(0, GROUP, 2):
-            first, second = lane == k, lane == k + 1
-            top_0, top_1 = top[:, k : k + 1], top[:, k + 1 : k + 2]
-            rest_0, rest_1 = rest[:, k : k + 1], rest[:, k + 1 : k + 2]
-            corner, upper = top_0[k : k + 1], top_1[k : k + 1]
-            lower, other = top_0[k + 1 : k + 2], top_1[k + 1 : k + 2]
-            inverse = 1.0 / (corner * other - upper * lower)
-            row_0 = jnp.where(first, 1.0, jnp.where(second, 0.0, top[k : k + 1]))
-            row_1 = jnp.where(first, 0.0, jnp.where(second, 1.0, top[k + 1 : k + 2]))
-            new_0 = (other * row_0 - upper * row_1) * inverse
-            new_1 = (corner * row_1 - lower * row_0) * inverse
-            both = first | second
-            at_0, at_1 = row_id == k, row_id == k + 1
-            top_0 = jnp.where(at_0, -1.0, jnp.where(at_1, 0.0, top_0))
-            top_1 = jnp.where(at_1, -1.0, jnp.where(at_0, 0.0, top_1))
-            top = jnp.where(both | at_0 | at_1, 0.0, top) - top_0 * new_0 - top_1 * new_1
-            rest = jnp.where(both, 0.0, rest) - rest_0 * new_0 - rest_1 * new_1
-        return pltpu.roll(jnp.concatenate([rest, top], axis=0), size - GROUP, 1)
-
-    return lax.fori_loop(0, size // GROUP, group, block)
+        columns = [jnp.broadcast_to(top[:, j : j + 1], (GROUP, size)) for j in range(GROUP)]
+        for k in range(GROUP):
+            at_k = row_id == k
+            pivot = 1.0 / columns[k][k : k + 1]
+            old = jnp.where(at_k, -1.0, columns[k]) * pivot
+            for j in range(GROUP):
+                if j != k:
+                    columns[j] = jnp.where(at_k, 0.0, columns[j]) - old * columns[j][k : k + 1]
+            columns[k] = -old
+        rows = jnp.zeros((GROUP, size), jnp.float32)
+        for j in range(GROUP):
+            rows = rows + columns[j] * jnp.where(
+                inside, jnp.where(lane == j, 1.0, 0.0), top[j : j + 1]
+            )
+        left = rest
+        rest = jnp.where(inside, 0.0, rest)
+        for j in range(GROUP):
+            rest = rest - left[:, j : j + 1] * rows[j : j + 1]
+        return pltpu.roll(jnp.concatenate([rest, rows], axis=0), size - GROUP, 1)
+
+    return lax.fori_loop(0, size // GROUP, group, block, unroll=2)
 
 
 def solve_kernel(count, feature_count, tiles_ref, half_ref, scale_ref, right, *strips):
@@ -219,7 +222,7 @@
             jax.ShapeDtypeStruct((build_grads.shape[0] * dp_parts, span), jnp.bfloat16),
         ),
         in_specs=[anywhere] * 2,
-        out_specs=(anywhere, anywhere),
+        out_specs=(anywhere, pl.BlockSpec(memory_space=pltpu.VMEM)),
         scratch_shapes=[
             pltpu.SemaphoreType.DMA((2,)),
             pltpu.SemaphoreType.DMA((parts,)),
@@ -305,7 +308,7 @@
     feat, dp = lax.axis_index("feat"), lax.axis_index("dp")
     chips = dp_parts // 2
     core, chip = lax.rem(dp, 2), dp // 2
-    total = values_ref.shape[0]
+    total = values_ref.shape[0] // CHUNKS
     half, quarter, piece = total // 2, total // dp_parts, total // (dp_parts * feat_parts)
 
     def part(start, size):
@@ -344,47 +347,58 @@
         copy.start()
         return copy
 
-    send(values_ref.at[part((1 - core) * half, half)], pair_in, other).wait()
-    pair_sum[...] = values_ref[part(core * half, half), :] + pair_in[...]
-
-    copies = []
-    for step in range(1, chips):
-        at, device = along_chips(step)
-        copies.append(send(pair_sum.at[part(at * quarter, quarter)], chip_in.at[step - 1], device))
-    value = pair_sum[part(chip * quarter, quarter), :]
-    for step, copy in enumerate(copies):
-        copy.wait()
-        value = value + chip_in[step]
-    chip_sum[...] = value
-
-    copies = []
-    for step in range(1, feat_parts):
-        at, device = along_feat(step)
-        copies.append(send(chip_sum.at[part(at * piece, piece)], feat_in.at[step - 1], device))
-    value = chip_sum[part(feat * piece, piece), :]
-    for step, copy in enumerate(copies):
-        copy.wait()
-        value = value + feat_in[step]
-
-    base = core * half + chip * quarter
-    mine = whole_ref.at[part(base + feat * piece, piece)]
-    mine[...] = value
-    copies = [send(mine, mine, along_feat(step)[1]) for step in range(1, feat_parts)]
-    for copy in copies:
-        copy.wait()
-    mine = whole_ref.at[part(base, quarter)]
-    copies = [send(mine, mine, along_chips(step)[1]) for step in range(1, chips)]
-    for copy in copies:
-        copy.wait()
-    mine = whole_ref.at[part(core * half, half)]
-    send(mine, mine, other).wait()
+    chunks = range(CHUNKS)
+    base = [c * total + core * half + chip * quarter for c in chunks]
+    pair, along, across, gather, back, last = {}, {}, {}, {}, {}, {}
+    for c in chunks:
+        outgoing = values_ref.at[part(c * total + (1 - core) * half, half)]
+        pair[c] = send(outgoing, pair_in.at[c], other)
+    for c in chunks:
+        pair[c].wait()
+        pair_sum[c] = values_ref[part(c * total + core * half, half), :] + pair_in[c]
+        along[c] = []
+        for step in range(1, chips):
+            at, device = along_chips(step)
+            source = pair_sum.at[c, part(at * quarter, quarter)]
+            along[c].append(send(source, chip_in.at[c, step - 1], device))
+    for c in chunks:
+        value = pair_sum[c, part(chip * quarter, quarter), :]
+        for step, copy in enumerate(along[c]):
+            copy.wait()
+            value = value + chip_in[c, step]
+        chip_sum[c] = value
+        across[c] = []
+        for step in range(1, feat_parts):
+            at, device = along_feat(step)
+            source = chip_sum.at[c, part(at * piece, piece)]
+            across[c].append(send(source, feat_in.at[c, step - 1], device))
+    for c in chunks:
+        value = chip_sum[c, part(feat * piece, piece), :]
+        for step, copy in enumerate(across[c]):
+            copy.wait()
+            value = value + feat_in[c, step]
+        mine = whole_ref.at[part(base[c] + feat * piece, piece)]
+        mine[...] = value
+        gather[c] = [send(mine, mine, along_feat(step)[1]) for step in range(1, feat_parts)]
+    for c in chunks:
+        for copy in gather[c]:
+            copy.wait()
+        mine = whole_ref.at[part(base[c], quarter)]
+        back[c] = [send(mine, mine, along_chips(step)[1]) for step in range(1, chips)]
+    for c in chunks:
+        for copy in back[c]:
+            copy.wait()
+        mine = whole_ref.at[part(c * total + core * half, half)]
+        last[c] = send(mine, mine, other)
+    for c in chunks:
+        last[c].wait()
 
 
 def sum_everywhere(values, feat_parts, dp_parts):
-    total = values.shape[0]
+    total = values.shape[0] // CHUNKS
     chips = dp_parts // 2
     quarter, piece = total // dp_parts, total // (dp_parts * feat_parts)
-    copies = 2 * (1 + (chips - 1) + (feat_parts - 1))
+    copies = 2 * CHUNKS * (1 + (chips - 1) + (feat_parts - 1))
     vmem = pl.BlockSpec(memory_space=pltpu.VMEM)
     return pl.pallas_call(
         functools.partial(sum_kernel, feat_parts, dp_parts),
@@ -392,11 +406,11 @@
         in_specs=[vmem],
         out_specs=vmem,
         scratch_shapes=[
-            pltpu.VMEM((total // 2, BLOCK), jnp.float32),
-            pltpu.VMEM((total // 2, BLOCK), jnp.float32),
-            pltpu.VMEM((max(1, chips - 1), quarter, BLOCK), jnp.float32),
-            pltpu.VMEM((quarter, BLOCK), jnp.float32),
-            pltpu.VMEM((max(1, feat_parts - 1), piece, BLOCK), jnp.float32),
+            pltpu.VMEM((CHUNKS, total // 2, BLOCK), jnp.float32),
+            pltpu.VMEM((CHUNKS, total // 2, BLOCK), jnp.float32),
+            pltpu.VMEM((CHUNKS, max(1, chips - 1), quarter, BLOCK), jnp.float32),
+            pltpu.VMEM((CHUNKS, quarter, BLOCK), jnp.float32),
+            pltpu.VMEM((CHUNKS, max(1, feat_parts - 1), piece, BLOCK), jnp.float32),
             pltpu.SemaphoreType.DMA((copies,)),
             pltpu.SemaphoreType.DMA((copies,)),
         ],
@@ -594,7 +608,7 @@
     build_count, query_count = b_local.shape[0], q_local.shape[0]
     count, width = build_count // BLOCK, -(-query_count // BLOCK)
     used = count * (count + 1) // 2 + count * width + 1
-    unit = max(1, feat_parts * dp_parts // 16)
+    unit = max(1, feat_parts * dp_parts * CHUNKS // 16)
     tile_count = -(-used // unit) * unit
     tiles = gram_tiles(q_local, b_local, tile_count)
     whole = sum_everywhere(tiles, feat_parts, dp_parts).reshape(tile_count, BLOCK, BLOCK)

time: 192 us -> 148 us (0.77)
  Pallas kernels: 184 us -> 140 us
    pallas_call x1, Pallas kernels: 65.1 us -> 23 us  [solve(): pl.pallas_call(functools.partial(solve_kernel, count, feature_count), out...]
    pallas_call x1, Pallas kernels: 30.8 us -> 27.7 us  [sum_everywhere(): pl.pallas_call(functools.partial(sum_kernel, feat_parts, dp_parts), out_s...]
    pallas_call x1, Pallas kernels: 59 us -> 61 us  [exchange(): pl.pallas_call(functools.partial(exchange_kernel, feat_parts, dp_parts),...]
where the time goes in v2:
time: 148 us; the launch traced here: 147 us
  Pallas kernels  140 us (95%)
  local copies, waits for them, and re-layouts  7.18 us (5%)
    pallas_call x1, Pallas kernels, exchange(): pl.pallas_call(functools.partial(exchange_kernel, feat_parts, dp_parts),...  61 us
    pallas_call x1, Pallas kernels, sum_everywhere(): pl.pallas_call(functools.partial(sum_kernel, feat_parts, dp_parts), out_s...  27.7 us
    pallas_call x1, Pallas kernels, score(): pl.pallas_call(functools.partial(score_kernel, feat_parts, dp_parts), out...  23.8 us
    pallas_call x1, Pallas kernels, solve(): pl.pallas_call(functools.partial(solve_kernel, count, feature_count), out...  23 us
    pallas_call x1, Pallas kernels, gram_tiles(): pl.pallas_call(gram_kernel, out_shape=jax.ShapeDtypeStruct((tile_count *...  4.51 us

profile of v2, /device:TPU:0, one launch (start us, length us, event | category | flops | bytes accessed | tf_op | source)
XLA Modules:
  0.0 147.3 jit_solution(9459834483445872476)
XLA Ops:
  0.0 1.4 reshape.12
  1.4 0.5 copy.6
  1.9 1.2 reshape.13.query_ref
  3.1 61.0 %shard_map.37 = (bf16[32,64,128]{2,1,0:T(8,128)(2,1)}, bf16[512,4096]{1,0:T(8,128)(2,1)}) custom-call(bf16[32,64,128]{2,1,0:T(8,128)(2,1)} %reshape.13.query_ref, bf16[128,16384]{1,0:T(8,128)(2,1)} %build_ref.1), custom_call_target="tpu_custom_call" | custom-call | tf_op jit(solution)/shard_map/pallas_call | solution.py:218
  64.1 1.3 reshape.14.query_ref
  65.4 0.0 copy-start
  65.4 2.2 %copy-done = bf16[512,4096]{1,0:T(8,128)(2,1)S(1)} copy-done((bf16[512,4096]{1,0:T(8,128)(2,1)S(1)}, bf16[512,4096]{1,0:T(8,128)(2,1)}, u32[]{:S(2)}) %copy-start) | copy-done | bytes 4194328
  67.6 0.0 copy-start.1
  67.6 4.5 %shard_map.38.values_ref = f32[2048,128]{1,0:T(8,128)S(1)} custom-call(bf16[64,4096]{1,0:T(8,128)(2,1)S(1)} %reshape.14.query_ref, bf16[512,4096]{1,0:T(8,128)(2,1)S(1)} %copy-done), custom_call_target="tpu_custom_call" | custom-call | tf_op jit(solution)/shard_map/pallas_call | solution.py:290
  72.1 27.7 %shard_map.39 = f32[2048,128]{1,0:T(8,128)S(1)} custom-call(f32[2048,128]{1,0:T(8,128)S(1)} %shard_map.38.values_ref), custom_call_target="tpu_custom_call" | custom-call | tf_op jit(solution)/shard_map/pallas_call | solution.py:403
  99.8 23.0 %shard_map.40 = (bf16[512,128]{1,0:T(8,128)(2,1)S(1)}, f32[1,128]{1,0:T(1,128)S(1)}) custom-call(f32[16,128,128]{2,1,0:T(8,128)S(1)} %bitcast.4), custom_call_target="tpu_custom_call" | custom-call | tf_op jit(solution)/shard_map/pallas_call | solution.py:122
  122.9 0.0 copy-done.1
  122.9 23.8 %shard_map.41 = f32[64,64]{1,0:T(8,128)S(1)} custom-call(bf16[512,128]{1,0:T(8,128)(2,1)S(1)} %get-tuple-element.11.half_ref, f32[1,128]{1,0:T(1,128)S(1)} %get-tuple-element.12.scale_ref, bf16[64,4096]{1,0:T(8,128)(2,1)S(1)} %reshape.14.query_ref, bf16[512,4096]{1,0:T(8,128)(2,1)S(1)} %copy-done.1, bf16[512,16384]{1,0:T(8,128)(2,1)} %scored_ref.1), custom_call_target="tpu_custom_call" | custom-call | tf_op jit(solution)/shard_map/pallas_call | solution.py:578
  146.7 0.6 copy.8
Async XLA Ops:
  65.4 2.2 %copy-start = (bf16[512,4096]{1,0:T(8,128)(2,1)S(1)}, bf16[512,4096]{1,0:T(8,128)(2,1)}, u32[]{:S(2)}) copy-start(bf16[512,4096]{1,0:T(8,128)(2,1)} %get-tuple-element.10.build_ref) | copy-start | bytes 12582916
  67.6 55.3 %copy-start.1 = (bf16[512,4096]{1,0:T(8,128)(2,1)S(1)}, bf16[512,4096]{1,0:T(8,128)(2,1)}, u32[]{:S(2)}) copy-start(bf16[512,4096]{1,0:T(8,128)(2,1)} %get-tuple-element.10.build_ref) | copy-start | bytes 12582916

commit v3 on v2

--- a/solution.py
+++ b/solution.py
@@ -10,6 +10,7 @@
 BLOCK = 128
 GROUP = 8
 CHUNKS = 2
+PIECES = 4
 
 
 def contract_last(left, right):
@@ -115,24 +116,6 @@
         scale_ref[:, lanes(j)] = 1.0 / jnp.sqrt(damping * kept)
 
 
-def solve(tiles, build_count, query_count, feature_count):
-    count = build_count // BLOCK
-    wide = -(-query_count // BLOCK) * BLOCK
-    vmem = pl.BlockSpec(memory_space=pltpu.VMEM)
-    return pl.pallas_call(
-        functools.partial(solve_kernel, count, feature_count),
-        out_shape=(
-            jax.ShapeDtypeStruct((build_count, wide), jnp.bfloat16),
-            jax.ShapeDtypeStruct((1, wide), jnp.float32),
-        ),
-        in_specs=[vmem],
-        out_specs=(vmem, vmem),
-        scratch_shapes=[pltpu.VMEM((build_count, wide), jnp.float32)]
-        + [pltpu.VMEM((BLOCK, (count - k) * BLOCK + wide), jnp.float32) for k in range(count)],
-        compiler_params=pltpu.CompilerParams(vmem_limit_bytes=48 * 1024 * 1024),
-    )(tiles)
-
-
 MESH = pl.DeviceIdType.MESH
 
 
@@ -283,24 +266,6 @@
         out_ref[pl.ds(place * BLOCK + j, 1), :] = row
 
 
-def gram_tiles(query_local, build_local, tile_count):
-    build_count, query_count = build_local.shape[0], query_local.shape[0]
-    wide = -(-query_count // BLOCK) * BLOCK
-    vmem = pl.BlockSpec(memory_space=pltpu.VMEM)
-    return pl.pallas_call(
-        gram_kernel,
-        out_shape=jax.ShapeDtypeStruct((tile_count * BLOCK, BLOCK), jnp.float32),
-        in_specs=[vmem] * 2,
-        out_specs=vmem,
-        scratch_shapes=[
-            pltpu.VMEM((build_count, build_count), jnp.float32),
-            pltpu.VMEM((build_count, wide), jnp.float32),
-            pltpu.VMEM((query_count, 1), jnp.float32),
-        ],
-        compiler_params=pltpu.CompilerParams(vmem_limit_bytes=48 * 1024 * 1024),
-    )(query_local, build_local)
-
-
 def sum_kernel(
     feat_parts, dp_parts, values_ref, whole_ref,
     pair_in, pair_sum, chip_in, chip_sum, feat_in, send_sem, recv_sem,
@@ -323,14 +288,6 @@
     def along_feat(step):
         at = lax.rem(feat + step, feat_parts)
         return at, {"dp": dp, "feat": at}
-
-    barrier = pltpu.get_barrier_semaphore()
-    peers = [other]
-    peers += [along_chips(step)[1] for step in range(1, chips)]
-    peers += [along_feat(step)[1] for step in range(1, feat_parts)]
-    for device in peers:
-        pl.semaphore_signal(barrier, inc=1, device_id=device, device_id_type=MESH)
-    pl.semaphore_wait(barrier, len(peers))
 
     used = [0]
 
@@ -394,42 +351,16 @@
         last[c].wait()
 
 
-def sum_everywhere(values, feat_parts, dp_parts):
-    total = values.shape[0] // CHUNKS
-    chips = dp_parts // 2
-    quarter, piece = total // dp_parts, total // (dp_parts * feat_parts)
-    copies = 2 * CHUNKS * (1 + (chips - 1) + (feat_parts - 1))
-    vmem = pl.BlockSpec(memory_space=pltpu.VMEM)
-    return pl.pallas_call(
-        functools.partial(sum_kernel, feat_parts, dp_parts),
-        out_shape=jax.ShapeDtypeStruct(values.shape, jnp.float32),
-        in_specs=[vmem],
-        out_specs=vmem,
-        scratch_shapes=[
-            pltpu.VMEM((CHUNKS, total // 2, BLOCK), jnp.float32),
-            pltpu.VMEM((CHUNKS, total // 2, BLOCK), jnp.float32),
-            pltpu.VMEM((CHUNKS, max(1, chips - 1), quarter, BLOCK), jnp.float32),
-            pltpu.VMEM((CHUNKS, quarter, BLOCK), jnp.float32),
-            pltpu.VMEM((CHUNKS, max(1, feat_parts - 1), piece, BLOCK), jnp.float32),
-            pltpu.SemaphoreType.DMA((copies,)),
-            pltpu.SemaphoreType.DMA((copies,)),
-        ],
-        compiler_params=pltpu.CompilerParams(
-            collective_id=1, has_side_effects=True, vmem_limit_bytes=48 * 1024 * 1024
-        ),
-    )(values)
-
-
 def score_kernel(
-    feat_parts, dp_parts, half_ref, scale_ref, query_ref, build_ref, scored_ref, out_ref,
+    feat_parts, dp_parts, owners, loads, half_ref, scale_ref, query_ref, build_ref, out_ref,
     normed, scored, total, packed, arrived,
-    load_sem, pair_send, pair_recv, chip_send, chip_recv, pass_send, pass_recv, feat_send, feat_recv,
+    pair_send, pair_recv, chip_send, chip_recv, pass_send, pass_recv, feat_send, feat_recv,
 ):
     feat, dp = lax.axis_index("feat"), lax.axis_index("dp")
     chips = dp_parts // 2
     core, chip = lax.rem(dp, 2), dp // 2
     query_count, span = query_ref.shape
-    rows = scored_ref.shape[0]
+    rows = total.shape[0]
     pieces = normed.shape[0] // dp_parts
     size = span // pieces
     other = {"dp": chip * 2 + 1 - core, "feat": feat}
@@ -443,23 +374,6 @@
     def along_feat(step):
         at = lax.rem(feat + step, feat_parts)
         return at, {"dp": dp, "feat": at}
-
-    loads = []
-    owners = [dp, chip * 2 + 1 - core]
-    for step in range(1, chips):
-        owners += [from_chip(step) + core, from_chip(step) + 1 - core]
-    for at, owner in enumerate(owners):
-        columns = pl.ds(pl.multiple_of(owner * span, BLOCK), span)
-        load = pltpu.make_async_copy(scored_ref.at[:, columns], scored.at[at], load_sem.at[at])
-        load.start()
-        loads.append(load)
-
-    peers = [other] + [along_chips(step) for step in range(1, chips)]
-    peers += [along_feat(step)[1] for step in range(1, feat_parts)]
-    barrier = pltpu.get_barrier_semaphore()
-    for device in peers:
-        pl.semaphore_signal(barrier, inc=1, device_id=device, device_id_type=MESH)
-    pl.semaphore_wait(barrier, len(peers))
 
     def send(slot, device, send_sem, recv_sem):
         return pltpu.make_async_remote_copy(
@@ -565,55 +479,133 @@
         ]
 
 
-def score(solved_half, scale, query_local, build_local, scored_grads, feat_parts, dp_parts):
+class Tiles:
+    def __init__(self, ref):
+        self.ref = ref
+
+    def __getitem__(self, at):
+        return self.ref[at * BLOCK : (at + 1) * BLOCK, :]
+
+
+def main_kernel(
+    feat_parts, dp_parts, feature_count, sizes, query_ref, build_ref, scored_ref, out_ref, *scratch
+):
+    scratch = list(scratch)
+    groups = []
+    for size in sizes:
+        groups.append(scratch[:size])
+        scratch = scratch[size:]
+    (tiles, whole, half, scale, load_sem), for_gram, for_sum, for_solve, for_score = groups
+    scored = for_score[1]
+    feat, dp = lax.axis_index("feat"), lax.axis_index("dp")
+    chips = dp_parts // 2
+    core, chip = lax.rem(dp, 2), dp // 2
+    span = query_ref.shape[1]
+
+    peers = [{"dp": chip * 2 + 1 - core, "feat": feat}]
+    owners = [dp, chip * 2 + 1 - core]
+    for step in range(1, chips):
+        peers.append({"dp": lax.rem(chip + step, chips) * 2 + core, "feat": feat})
+        sender = lax.rem(chip + chips - step, chips) * 2
+        owners += [sender + core, sender + 1 - core]
+    for step in range(1, feat_parts):
+        peers.append({"dp": dp, "feat": lax.rem(feat + step, feat_parts)})
+    barrier = pltpu.get_barrier_semaphore()
+    for device in peers:
+        pl.semaphore_signal(barrier, inc=1, device_id=device, device_id_type=MESH)
+
+    loads = []
+    for at, owner in enumerate(owners):
+        columns = pl.ds(pl.multiple_of(owner * span, BLOCK), span)
+        load = pltpu.make_async_copy(scored_ref.at[:, columns], scored.at[at], load_sem.at[at])
+        load.start()
+        loads.append(load)
+
+    gram_kernel(query_ref, build_ref, tiles, *for_gram)
+    pl.semaphore_wait(barrier, len(peers))
+    sum_kernel(feat_parts, dp_parts, tiles, whole, *for_sum)
+    count = build_ref.shape[0] // BLOCK
+    solve_kernel(count, feature_count, Tiles(whole), half, scale, *for_solve)
+    score_kernel(
+        feat_parts, dp_parts, owners, loads, half, scale, query_ref, build_ref, out_ref, *for_score
+    )
+
+
+def influence(query_local, build_local, scored_grads, feature_count, feat_parts, dp_parts):
     query_count, span = query_local.shape
+    build_count = build_local.shape[0]
     rows = scored_grads.shape[0]
-    pieces = 2 if span % (2 * BLOCK) == 0 else 1
+    count, width = build_count // BLOCK, -(-query_count // BLOCK)
+    wide = width * BLOCK
+    used = count * (count + 1) // 2 + count * width + 1
+    unit = max(1, feat_parts * dp_parts * CHUNKS // 16)
+    flat = -(-used // unit) * unit * BLOCK
     chips = dp_parts // 2
+    chunk = flat // CHUNKS
+    quarter, piece = chunk // dp_parts, chunk // (dp_parts * feat_parts)
+    copies = 2 * CHUNKS * (1 + (chips - 1) + (feat_parts - 1))
+    pieces = PIECES if span % (PIECES * BLOCK) == 0 else 1
     share = rows // feat_parts
     fold = BLOCK // query_count if query_count < BLOCK and share % (8 * BLOCK // query_count) == 0 else 1
-    vmem = pl.BlockSpec(memory_space=pltpu.VMEM)
     remote = max(1, (chips - 1) * pieces)
-    dma = pltpu.SemaphoreType.DMA
+    vmem, dma = pltpu.VMEM, pltpu.SemaphoreType.DMA
+    shared = [
+        vmem((flat, BLOCK), jnp.float32),
+        vmem((flat, BLOCK), jnp.float32),
+        vmem((build_count, wide), jnp.bfloat16),
+        vmem((1, wide), jnp.float32),
+        dma((dp_parts,)),
+    ]
+    for_gram = [
+        vmem((build_count, build_count), jnp.float32),
+        vmem((build_count, wide), jnp.float32),
+        vmem((query_count, 1), jnp.float32),
+    ]
+    for_sum = [
+        vmem((CHUNKS, chunk // 2, BLOCK), jnp.float32),
+        vmem((CHUNKS, chunk // 2, BLOCK), jnp.float32),
+        vmem((CHUNKS, max(1, chips - 1), quarter, BLOCK), jnp.float32),
+        vmem((CHUNKS, quarter, BLOCK), jnp.float32),
+        vmem((CHUNKS, max(1, feat_parts - 1), piece, BLOCK), jnp.float32),
+        dma((copies,)),
+        dma((copies,)),
+    ]
+    for_solve = [vmem((build_count, wide), jnp.float32)]
+    for_solve += [vmem((BLOCK, (count - k) * BLOCK + wide), jnp.float32) for k in range(count)]
+    for_score = [
+        vmem((dp_parts * pieces, query_count, span // pieces), jnp.bfloat16),
+        vmem((dp_parts, rows, span), jnp.bfloat16),
+        vmem((rows, query_count), jnp.float32),
+        vmem((feat_parts, share // fold, query_count * fold), jnp.float32),
+        vmem((max(1, feat_parts - 1), share // fold, query_count * fold), jnp.float32),
+        dma((pieces,)),
+        dma((pieces,)),
+        dma((remote,)),
+        dma((remote,)),
+        dma((remote,)),
+        dma((remote,)),
+        dma((feat_parts,)),
+        dma((feat_parts,)),
+    ]
+    groups = [shared, for_gram, for_sum, for_solve, for_score]
+    sizes = [len(group) for group in groups]
+    inside = pl.BlockSpec(memory_space=pltpu.VMEM)
     return pl.pallas_call(
-        functools.partial(score_kernel, feat_parts, dp_parts),
+        functools.partial(main_kernel, feat_parts, dp_parts, feature_count, sizes),
         out_shape=jax.ShapeDtypeStruct((share, query_count), jnp.float32),
-        in_specs=[vmem] * 4 + [pl.BlockSpec(memory_space=pl.ANY)],
-        out_specs=vmem,
-        scratch_shapes=[
-            pltpu.VMEM((dp_parts * pieces, query_count, span // pieces), jnp.bfloat16),
-            pltpu.VMEM((dp_parts, rows, span), jnp.bfloat16),
-            pltpu.VMEM((rows, query_count), jnp.float32),
-            pltpu.VMEM((feat_parts, share // fold, query_count * fold), jnp.float32),
-            pltpu.VMEM((max(1, feat_parts - 1), share // fold, query_count * fold), jnp.float32),
-            dma((dp_parts,)),
-            dma((pieces,)),
-            dma((pieces,)),
-            dma((remote,)),
-            dma((remote,)),
-            dma((remote,)),
-            dma((remote,)),
-            dma((feat_parts,)),
-            dma((feat_parts,)),
-        ],
+        in_specs=[inside, inside, pl.BlockSpec(memory_space=pl.ANY)],
+        out_specs=inside,
+        scratch_shapes=sum(groups, []),
         compiler_params=pltpu.CompilerParams(
-            collective_id=2, has_side_effects=True, vmem_limit_bytes=48 * 1024 * 1024
+            collective_id=1, has_side_effects=True, vmem_limit_bytes=52 * 1024 * 1024
         ),
-    )(solved_half, scale, query_local, build_local, scored_grads)
+    )(query_local, build_local, scored_grads)
 
 
 def on_device(feat_parts, dp_parts, query_grads, build_grads, scored_grads):
+    q_local, b_local = exchange(query_grads, build_grads, feat_parts, dp_parts)
     feature_count = query_grads.shape[1]
-    q_local, b_local = exchange(query_grads, build_grads, feat_parts, dp_parts)
-    build_count, query_count = b_local.shape[0], q_local.shape[0]
-    count, width = build_count // BLOCK, -(-query_count // BLOCK)
-    used = count * (count + 1) // 2 + count * width + 1
-    unit = max(1, feat_parts * dp_parts * CHUNKS // 16)
-    tile_count = -(-used // unit) * unit
-    tiles = gram_tiles(q_local, b_local, tile_count)
-    whole = sum_everywhere(tiles, feat_parts, dp_parts).reshape(tile_count, BLOCK, BLOCK)
-    solved_half, scale = solve(whole, build_count, query_count, feature_count)
-    return score(solved_half, scale, q_local, b_local, scored_grads, feat_parts, dp_parts)
+    return influence(q_local, b_local, scored_grads, feature_count, feat_parts, dp_parts)
 
 
 def solution(mesh):

time: 148 us -> 145 us (0.980)
  local copies, waits for them, and re-layouts: 7.18 us -> 4.98 us
    unnamed x5 -> x1, local copies, waits for them, and re-layouts: 2.8 us -> 0.62 us
    pallas_call x4 -> x1, Pallas kernels: 79.1 us -> 78.5 us  [influence(): pl.pallas_call(functools.partial(main_kernel, feat_parts, dp_parts, featu...]
where the time goes in v3:
time: 145 us; the launch traced here: 144 us
  Pallas kernels  139 us (96%)
  local copies, waits for them, and re-layouts  4.98 us (3%)
    pallas_call x1, Pallas kernels, influence(): pl.pallas_call(functools.partial(main_kernel, feat_parts, dp_parts, featu...  78.5 us
    pallas_call x1, Pallas kernels, exchange(): pl.pallas_call(functools.partial(exchange_kernel, feat_parts, dp_parts),...  61 us

profile of v3, /device:TPU:0, one launch (start us, length us, event | category | flops | bytes accessed | tf_op | source)
XLA Modules:
  0.0 144.4 jit_solution(7454325133497567486)
XLA Ops:
  0.0 1.4 reshape.9
  1.4 0.5 copy.6
  1.9 1.2 reshape.10.query_ref
  3.1 61.0 %shard_map.37 = (bf16[32,64,128]{2,1,0:T(8,128)(2,1)}, bf16[512,4096]{1,0:T(8,128)(2,1)}) custom-call(bf16[32,64,128]{2,1,0:T(8,128)(2,1)} %reshape.10.query_ref, bf16[128,16384]{1,0:T(8,128)(2,1)} %build_ref.1), custom_call_target="tpu_custom_call" | custom-call | tf_op jit(solution)/shard_map/pallas_call | solution.py:201
  64.1 1.3 reshape.11.query_ref
  65.4 78.5 %shard_map.38 = f32[64,64]{1,0:T(8,128)S(1)} custom-call(bf16[64,4096]{1,0:T(8,128)(2,1)S(1)} %reshape.11.query_ref, bf16[512,4096]{1,0:T(8,128)(2,1)} %get-tuple-element.8.build_ref, bf16[512,16384]{1,0:T(8,128)(2,1)} %scored_ref.1), custom_call_target="tpu_custom_call" | custom-call | tf_op jit(solution)/shard_map/pallas_call | solution.py:593
  143.8 0.6 copy.8
